TPU v7x, 256 devices: a whole 4x4x8 slice. The times are simulated.
256 devices in a mesh: pts: 256 (over z, y, x, core).
Axes of the slice: x: 4, y: 4, z: 8, core: 2. Of those that a mesh axis runs over, the one named last changes fastest.
Arguments:
- points: float32 [64, 524288], P(None, 'pts'), may hold values from -6 to 6
- probes: float32 [32, 524288], P(None, 'pts'), may hold values from -0.078125 to 0.078125
- inv_length: float32 [64], replicated, may hold values from 0.03 to 0.6
- partners: int32 [2, 256], replicated, may hold values from 0 to 255, as said below
Outputs:
- product: float32 [32, 524288], P(None, 'pts')
Inputs may be any that keep to these rules, and one draw needn't show every extreme that they name: partners[r, i] = i XOR m_r, with masks m_r of 1 to 255 that differ between rounds; so every round pairs the blocks two by two.
All inputs are finite; a program needn't handle non-finite values.
Results may differ from a plain program's by a relative error of at most 0.0003.
Values sent between devices are 32-bit elements; how exact they have to be, the bound alone decides.
A program may use at most 64 MiB of HBM per device.

v0:
```python
import jax
import jax.numpy as jnp
from jax import lax
from jax.sharding import PartitionSpec as P

ROUNDS = 2


root_five = 5.0**0.5


def partner(block, axis, distance):
    count = lax.axis_size(axis)
    route = []
    for low in range(count):
        high = low | 1 << distance
        if high != low and high < count:
            route += [(low, high), (high, low)]
    return lax.ppermute(block, axis, route)


def matern(left, right):
    inner = lax.dot_general(
        left,
        right,
        (((0,), (0,)), ((), ())),
        precision=lax.Precision.HIGHEST,
        preferred_element_type=jnp.float32,
    )
    left_sq = jnp.sum(left * left, axis=0)
    right_sq = jnp.sum(right * right, axis=0)
    dist_sq = jnp.maximum(left_sq[:, None] + right_sq[None, :] - 2.0 * inner, 0.0)
    scaled_dist = root_five * jnp.sqrt(dist_sq)
    return (1.0 + scaled_dist + scaled_dist * scaled_dist / 3.0) * jnp.exp(-scaled_dist)


def split_rows(array, step):
    return array.reshape(array.shape[0], array.shape[1] // step, step).transpose(1, 0, 2)


def join_rows(pieces):
    return pieces.transpose(1, 0, 2).reshape(pieces.shape[1], pieces.shape[0] * pieces.shape[2])


def block_terms(left, right, weights):
    step = min(256, left.shape[1])

    def one_piece(piece):
        kernel = matern(piece, right)
        return lax.dot_general(
            weights,
            kernel,
            (((1,), (1,)), ((), ())),
            precision=lax.Precision.HIGHEST,
            preferred_element_type=jnp.float32,
        )

    return join_rows(lax.map(one_piece, split_rows(left, step)))


def route_pair(pair, mask):
    levels = lax.axis_size("pts").bit_length() - 1
    for level in range(levels):
        flag = jnp.bitwise_and(jnp.right_shift(mask, level), 1) == 1

        def moving(operand, level=level):
            return partner(operand, "pts", level)

        def staying(operand):
            return operand

        pair = lax.cond(flag, moving, staying, pair)
    return pair


def body(points, probes, inv_length, partners):
    scaled = points * inv_length[:, None]
    masks = partners[:, 0]
    total = block_terms(scaled, scaled, probes)
    for round_index in range(ROUNDS):
        far_points, far_probes = route_pair((scaled, probes), masks[round_index])
        total = total + block_terms(scaled, far_points, far_probes)
    return total


def solution(mesh):
    in_specs = (P(None, "pts"), P(None, "pts"), P(), P())
    out_specs = P(None, "pts")
    return jax.shard_map(body, mesh=mesh, in_specs=in_specs, out_specs=out_specs, check_vma=False)
```

profile of v0, /device:TPU:1, one launch (start us, length us, event | category | flops | bytes accessed | tf_op | source)
XLA Modules:
  0.0 328.9 jit_solution(4465924401806168486)
XLA Ops:
  8.6 21.6 %conditional.26 = ((f32[64,2048]{1,0:T(8,128)}, f32[32,2048]{1,0:T(8,128)})) conditional(s32[]{:T(128)} %bitcast.23, (f32[64,2048]{1,0:T(8,128)}, f32[32,2048]{1,0:T(8,128)}) %get-tuple-element.716, (f32[64,2048]{1,0:T(8,128)}, f32[32,2048]{1,0:T(8,128)}) %get-tuple-element.716), branch_computations={%region_29.30_spmd, %region_30.31_spmd} | conditional | bytes 4718696 | solution.py:72
  12.2 16.5 %collective-permute-done.19 = f32[32,2048]{1,0:T(8,128)S(1)} collective-permute-done((f32[32,2048]{1,0:T(8,128)}, f32[32,2048]{1,0:T(8,128)S(1)}, u32[]{:S(2)}, u32[]{:S(2)}) %collective-permute-start.19) | collective-permute-done | bytes 262176 | tf_op jit(solution)/shard_map/cond/branch_1_fun/ppermute | solution.py:19
  30.2 21.7 %conditional.28 = ((f32[64,2048]{1,0:T(8,128)}, f32[32,2048]{1,0:T(8,128)})) conditional(s32[]{:T(128)} %bitcast.21, (f32[64,2048]{1,0:T(8,128)}, f32[32,2048]{1,0:T(8,128)}) %get-tuple-element.718, (f32[64,2048]{1,0:T(8,128)}, f32[32,2048]{1,0:T(8,128)}) %get-tuple-element.718), branch_computations={%region_33.34_spmd, %region_34.35_spmd} | conditional | bytes 4718696 | solution.py:72
  30.2 3.8 %collective-permute-start.22 = (f32[64,2048]{1,0:T(8,128)}, f32[64,2048]{1,0:T(8,128)S(1)}, u32[]{:S(2)}, u32[]{:S(2)}) collective-permute-start(f32[64,2048]{1,0:T(8,128)} %get-tuple-element.355), channel_id=1, source_target_pairs={{0,16},{16,0},{1,17},{17,1},{2,18},{18,2},{3,19},{19,3},{4,20},{20... | collective-permute-start | bytes 1572872 | tf_op jit(solution)/shard_map/cond/branch_1_fun/ppermute | solution.py:19
  34.0 16.4 %collective-permute-done.23 = f32[32,2048]{1,0:T(8,128)S(1)} collective-permute-done((f32[32,2048]{1,0:T(8,128)}, f32[32,2048]{1,0:T(8,128)S(1)}, u32[]{:S(2)}, u32[]{:S(2)}) %collective-permute-start.23) | collective-permute-done | bytes 262176 | tf_op jit(solution)/shard_map/cond/branch_1_fun/ppermute | solution.py:19
  53.2 54.8 %while.38 = (s32[]{:T(128)}, f32[8,32,256]{2,1,0:T(8,128)S(1)}, f32[8,64,256]{2,1,0:T(8,128)S(1)}, f32[2048]{0:T(1024)S(1)}, f32[64,2048]{1,0:T(8,128)}, /*index=5*/f32[32,2048]{1,0:T(8,128)}, s32[]{:T(128)}) while((s32[]{:T(128)}, f32[8,32,256]{2,1,0:T(8,128)S(1)}, f32[8,64,256]{2,1,0:T(8,128)S(1)}, f32[2048]{0:T(1024)S(1)}, ...), condition=%wide.region_45.46_spmd, body=%wide.region_43.45_spmd.sunk | while | flops 609779456 | bytes 5154913 | solution.py:58
  53.3 3.6 %fusion.129 = f32[256,2048]{1,0:T(8,128)S(1)} fusion(f32[64,2048]{1,0:T(8,128)} %get-tuple-element.629, f32[2048]{0:T(1024)S(1)} %get-tuple-element.628, f32[256]{0:T(256)S(1)} %fusion.128, f32[8,64,256]{2,1,0:T(8,128)S(1)} %get-tuple-element.627, s32[]{:T(128)S(6)} %copy.53), kind=kOutput, calls=%fused_computation.52.clone.1 | convolution fusion | flops 405274624 | bytes 2696196 | tf_op jit(solution)/shard_map/while/body/eval_jaxpr/dot_general | solution.py:23
  60.1 3.6 %fusion.129 = f32[256,2048]{1,0:T(8,128)S(1)} fusion(f32[64,2048]{1,0:T(8,128)} %get-tuple-element.629, f32[2048]{0:T(1024)S(1)} %get-tuple-element.628, f32[256]{0:T(256)S(1)} %fusion.128, f32[8,64,256]{2,1,0:T(8,128)S(1)} %get-tuple-element.627, s32[]{:T(128)S(6)} %copy.53), kind=kOutput, calls=%fused_computation.52.clone.1 | convolution fusion | flops 405274624 | bytes 2696196 | tf_op jit(solution)/shard_map/while/body/eval_jaxpr/dot_general | solution.py:23
  67.0 3.6 %fusion.129 = f32[256,2048]{1,0:T(8,128)S(1)} fusion(f32[64,2048]{1,0:T(8,128)} %get-tuple-element.629, f32[2048]{0:T(1024)S(1)} %get-tuple-element.628, f32[256]{0:T(256)S(1)} %fusion.128, f32[8,64,256]{2,1,0:T(8,128)S(1)} %get-tuple-element.627, s32[]{:T(128)S(6)} %copy.53), kind=kOutput, calls=%fused_computation.52.clone.1 | convolution fusion | flops 405274624 | bytes 2696196 | tf_op jit(solution)/shard_map/while/body/eval_jaxpr/dot_general | solution.py:23
  73.8 3.6 %fusion.129 = f32[256,2048]{1,0:T(8,128)S(1)} fusion(f32[64,2048]{1,0:T(8,128)} %get-tuple-element.629, f32[2048]{0:T(1024)S(1)} %get-tuple-element.628, f32[256]{0:T(256)S(1)} %fusion.128, f32[8,64,256]{2,1,0:T(8,128)S(1)} %get-tuple-element.627, s32[]{:T(128)S(6)} %copy.53), kind=kOutput, calls=%fused_computation.52.clone.1 | convolution fusion | flops 405274624 | bytes 2696196 | tf_op jit(solution)/shard_map/while/body/eval_jaxpr/dot_general | solution.py:23
  80.7 3.6 %fusion.129 = f32[256,2048]{1,0:T(8,128)S(1)} fusion(f32[64,2048]{1,0:T(8,128)} %get-tuple-element.629, f32[2048]{0:T(1024)S(1)} %get-tuple-element.628, f32[256]{0:T(256)S(1)} %fusion.128, f32[8,64,256]{2,1,0:T(8,128)S(1)} %get-tuple-element.627, s32[]{:T(128)S(6)} %copy.53), kind=kOutput, calls=%fused_computation.52.clone.1 | convolution fusion | flops 405274624 | bytes 2696196 | tf_op jit(solution)/shard_map/while/body/eval_jaxpr/dot_general | solution.py:23
  87.5 3.6 %fusion.129 = f32[256,2048]{1,0:T(8,128)S(1)} fusion(f32[64,2048]{1,0:T(8,128)} %get-tuple-element.629, f32[2048]{0:T(1024)S(1)} %get-tuple-element.628, f32[256]{0:T(256)S(1)} %fusion.128, f32[8,64,256]{2,1,0:T(8,128)S(1)} %get-tuple-element.627, s32[]{:T(128)S(6)} %copy.53), kind=kOutput, calls=%fused_computation.52.clone.1 | convolution fusion | flops 405274624 | bytes 2696196 | tf_op jit(solution)/shard_map/while/body/eval_jaxpr/dot_general | solution.py:23
  94.4 3.6 %fusion.129 = f32[256,2048]{1,0:T(8,128)S(1)} fusion(f32[64,2048]{1,0:T(8,128)} %get-tuple-element.629, f32[2048]{0:T(1024)S(1)} %get-tuple-element.628, f32[256]{0:T(256)S(1)} %fusion.128, f32[8,64,256]{2,1,0:T(8,128)S(1)} %get-tuple-element.627, s32[]{:T(128)S(6)} %copy.53), kind=kOutput, calls=%fused_computation.52.clone.1 | convolution fusion | flops 405274624 | bytes 2696196 | tf_op jit(solution)/shard_map/while/body/eval_jaxpr/dot_general | solution.py:23
  101.3 3.6 %fusion.129 = f32[256,2048]{1,0:T(8,128)S(1)} fusion(f32[64,2048]{1,0:T(8,128)} %get-tuple-element.629, f32[2048]{0:T(1024)S(1)} %get-tuple-element.628, f32[256]{0:T(256)S(1)} %fusion.128, f32[8,64,256]{2,1,0:T(8,128)S(1)} %get-tuple-element.627, s32[]{:T(128)S(6)} %copy.53), kind=kOutput, calls=%fused_computation.52.clone.1 | convolution fusion | flops 405274624 | bytes 2696196 | tf_op jit(solution)/shard_map/while/body/eval_jaxpr/dot_general | solution.py:23
  108.1 39.1 %while.36 = (s32[]{:T(128)}, f32[8,32,256]{2,1,0:T(8,128)S(1)}, f32[8,64,256]{2,1,0:T(8,128)S(1)}, f32[2048]{0:T(1024)S(1)}, f32[64,2048]{1,0:T(8,128)S(1)}, /*index=5*/f32[32,2048]{1,0:T(8,128)S(1)}, s32[]{:T(128)}) while((s32[]{:T(128)}, f32[8,32,256]{2,1,0:T(8,128)S(1)}, f32[8,64,256]{2,1,0:T(8,128)S(1)}, f32[2048]{0:T(1024)S(1)}, ...), condition=%wide.region_3.4_spmd, body=%wide.region_1.3_spmd.sunk | while | flops 609779456 | bytes 5154913 | solution.py:58
  153.7 19.9 %conditional.18 = ((f32[64,2048]{1,0:T(8,128)}, f32[32,2048]{1,0:T(8,128)})) conditional(s32[]{:T(128)} %bitcast.15, (f32[64,2048]{1,0:T(8,128)}, f32[32,2048]{1,0:T(8,128)}) %get-tuple-element.710, (f32[64,2048]{1,0:T(8,128)}, f32[32,2048]{1,0:T(8,128)}) %get-tuple-element.710), branch_computations={%region_8.9_spmd, %region_9.10_spmd} | conditional | bytes 4718696 | solution.py:72
  156.7 15.5 %collective-permute-done.5 = f32[32,2048]{1,0:T(8,128)S(1)} collective-permute-done((f32[32,2048]{1,0:T(8,128)}, f32[32,2048]{1,0:T(8,128)S(1)}, u32[]{:S(2)}, u32[]{:S(2)}) %collective-permute-start.5) | collective-permute-done | bytes 262176 | tf_op jit(solution)/shard_map/cond/branch_1_fun/ppermute | solution.py:19
  173.7 19.0 %conditional.20 = ((f32[64,2048]{1,0:T(8,128)}, f32[32,2048]{1,0:T(8,128)})) conditional(s32[]{:T(128)} %bitcast.13, (f32[64,2048]{1,0:T(8,128)}, f32[32,2048]{1,0:T(8,128)}) %get-tuple-element.712, (f32[64,2048]{1,0:T(8,128)}, f32[32,2048]{1,0:T(8,128)}) %get-tuple-element.712), branch_computations={%region_12.13_spmd, %region_13.14_spmd} | conditional | bytes 4718696 | solution.py:72
  176.7 14.6 %collective-permute-done.9 = f32[32,2048]{1,0:T(8,128)S(1)} collective-permute-done((f32[32,2048]{1,0:T(8,128)}, f32[32,2048]{1,0:T(8,128)S(1)}, u32[]{:S(2)}, u32[]{:S(2)}) %collective-permute-start.9) | collective-permute-done | bytes 262176 | tf_op jit(solution)/shard_map/cond/branch_1_fun/ppermute | solution.py:19
  192.7 37.7 %conditional.22 = ((f32[64,2048]{1,0:T(8,128)}, f32[32,2048]{1,0:T(8,128)})) conditional(s32[]{:T(128)} %bitcast.11, (f32[64,2048]{1,0:T(8,128)}, f32[32,2048]{1,0:T(8,128)}) %get-tuple-element.714, (f32[64,2048]{1,0:T(8,128)}, f32[32,2048]{1,0:T(8,128)}) %get-tuple-element.714), branch_computations={%region_16.17_spmd, %region_17.18_spmd} | conditional | bytes 4718696 | solution.py:72
  195.3 33.6 %collective-permute-done.13 = f32[32,2048]{1,0:T(8,128)S(1)} collective-permute-done((f32[32,2048]{1,0:T(8,128)}, f32[32,2048]{1,0:T(8,128)S(1)}, u32[]{:S(2)}, u32[]{:S(2)}) %collective-permute-start.13) | collective-permute-done | bytes 262176 | tf_op jit(solution)/shard_map/cond/branch_1_fun/ppermute | solution.py:19
  230.4 43.0 %conditional.23 = (f32[64,2048]{1,0:T(8,128)}, f32[32,2048]{1,0:T(8,128)}, bf16[64,2048]{1,0:T(8,128)(2,1)S(1)}, f32[2048]{0:T(1024)S(1)}) conditional(s32[]{:T(128)} %bitcast.10, (f32[64,2048]{1,0:T(8,128)}, f32[32,2048]{1,0:T(8,128)}) %get-tuple-element.715, (f32[64,2048]{1,0:T(8,128)}, f32[32,2048]{1,0:T(8,128)}) %get-tuple-element.715), branch_computations={%region_18.20_spmd, %region_20.22_spmd} | conditional | flops 391168 | bytes 5513328 | solution.py:72
  230.4 7.2 %collective-permute-start.28 = (f32[64,2048]{1,0:T(8,128)}, f32[64,2048]{1,0:T(8,128)S(1)}, u32[]{:S(2)}, u32[]{:S(2)}) collective-permute-start(f32[64,2048]{1,0:T(8,128)} %get-tuple-element.338), channel_id=1, source_target_pairs={{0,128},{128,0},{1,129},{129,1},{2,130},{130,2},{3,131},{131,3},{4... | collective-permute-start | bytes 1572872 | tf_op jit(solution)/shard_map/cond/branch_1_fun/ppermute | solution.py:19
  237.6 34.2 %collective-permute-done.29 = f32[32,2048]{1,0:T(8,128)S(1)} collective-permute-done((f32[32,2048]{1,0:T(8,128)}, f32[32,2048]{1,0:T(8,128)S(1)}, u32[]{:S(2)}, u32[]{:S(2)}) %collective-permute-start.29) | collective-permute-done | bytes 262176 | tf_op jit(solution)/shard_map/cond/branch_1_fun/ppermute | solution.py:19
  273.4 54.8 %while.37 = (s32[]{:T(128)}, f32[8,32,256]{2,1,0:T(8,128)S(1)}, f32[8,64,256]{2,1,0:T(8,128)S(1)}, f32[2048]{0:T(1024)S(1)}, f32[64,2048]{1,0:T(8,128)}, /*index=5*/f32[32,2048]{1,0:T(8,128)}, s32[]{:T(128)}) while((s32[]{:T(128)}, f32[8,32,256]{2,1,0:T(8,128)S(1)}, f32[8,64,256]{2,1,0:T(8,128)S(1)}, f32[2048]{0:T(1024)S(1)}, ...), condition=%wide.region_24.25_spmd, body=%wide.region_22.0_spmd.sunk | while | flops 609779456 | bytes 5154913 | solution.py:58
  273.4 3.6 %fusion.122 = f32[256,2048]{1,0:T(8,128)S(1)} fusion(f32[64,2048]{1,0:T(8,128)} %get-tuple-element.707, f32[2048]{0:T(1024)S(1)} %get-tuple-element.706, f32[256]{0:T(256)S(1)} %fusion.121, f32[8,64,256]{2,1,0:T(8,128)S(1)} %get-tuple-element.705, s32[]{:T(128)S(6)} %copy.101), kind=kOutput, calls=%fused_computation.28.clone.1 | convolution fusion | flops 405274624 | bytes 2696196 | tf_op jit(solution)/shard_map/while/body/eval_jaxpr/dot_general | solution.py:23
  280.3 3.6 %fusion.122 = f32[256,2048]{1,0:T(8,128)S(1)} fusion(f32[64,2048]{1,0:T(8,128)} %get-tuple-element.707, f32[2048]{0:T(1024)S(1)} %get-tuple-element.706, f32[256]{0:T(256)S(1)} %fusion.121, f32[8,64,256]{2,1,0:T(8,128)S(1)} %get-tuple-element.705, s32[]{:T(128)S(6)} %copy.101), kind=kOutput, calls=%fused_computation.28.clone.1 | convolution fusion | flops 405274624 | bytes 2696196 | tf_op jit(solution)/shard_map/while/body/eval_jaxpr/dot_general | solution.py:23
  287.1 3.6 %fusion.122 = f32[256,2048]{1,0:T(8,128)S(1)} fusion(f32[64,2048]{1,0:T(8,128)} %get-tuple-element.707, f32[2048]{0:T(1024)S(1)} %get-tuple-element.706, f32[256]{0:T(256)S(1)} %fusion.121, f32[8,64,256]{2,1,0:T(8,128)S(1)} %get-tuple-element.705, s32[]{:T(128)S(6)} %copy.101), kind=kOutput, calls=%fused_computation.28.clone.1 | convolution fusion | flops 405274624 | bytes 2696196 | tf_op jit(solution)/shard_map/while/body/eval_jaxpr/dot_general | solution.py:23
  300.8 3.6 %fusion.122 = f32[256,2048]{1,0:T(8,128)S(1)} fusion(f32[64,2048]{1,0:T(8,128)} %get-tuple-element.707, f32[2048]{0:T(1024)S(1)} %get-tuple-element.706, f32[256]{0:T(256)S(1)} %fusion.121, f32[8,64,256]{2,1,0:T(8,128)S(1)} %get-tuple-element.705, s32[]{:T(128)S(6)} %copy.101), kind=kOutput, calls=%fused_computation.28.clone.1 | convolution fusion | flops 405274624 | bytes 2696196 | tf_op jit(solution)/shard_map/while/body/eval_jaxpr/dot_general | solution.py:23
  307.7 3.6 %fusion.122 = f32[256,2048]{1,0:T(8,128)S(1)} fusion(f32[64,2048]{1,0:T(8,128)} %get-tuple-element.707, f32[2048]{0:T(1024)S(1)} %get-tuple-element.706, f32[256]{0:T(256)S(1)} %fusion.121, f32[8,64,256]{2,1,0:T(8,128)S(1)} %get-tuple-element.705, s32[]{:T(128)S(6)} %copy.101), kind=kOutput, calls=%fused_computation.28.clone.1 | convolution fusion | flops 405274624 | bytes 2696196 | tf_op jit(solution)/shard_map/while/body/eval_jaxpr/dot_general | solution.py:23
  314.5 3.6 %fusion.122 = f32[256,2048]{1,0:T(8,128)S(1)} fusion(f32[64,2048]{1,0:T(8,128)} %get-tuple-element.707, f32[2048]{0:T(1024)S(1)} %get-tuple-element.706, f32[256]{0:T(256)S(1)} %fusion.121, f32[8,64,256]{2,1,0:T(8,128)S(1)} %get-tuple-element.705, s32[]{:T(128)S(6)} %copy.101), kind=kOutput, calls=%fused_computation.28.clone.1 | convolution fusion | flops 405274624 | bytes 2696196 | tf_op jit(solution)/shard_map/while/body/eval_jaxpr/dot_general | solution.py:23
  321.4 3.6 %fusion.122 = f32[256,2048]{1,0:T(8,128)S(1)} fusion(f32[64,2048]{1,0:T(8,128)} %get-tuple-element.707, f32[2048]{0:T(1024)S(1)} %get-tuple-element.706, f32[256]{0:T(256)S(1)} %fusion.121, f32[8,64,256]{2,1,0:T(8,128)S(1)} %get-tuple-element.705, s32[]{:T(128)S(6)} %copy.101), kind=kOutput, calls=%fused_computation.28.clone.1 | convolution fusion | flops 405274624 | bytes 2696196 | tf_op jit(solution)/shard_map/while/body/eval_jaxpr/dot_general | solution.py:23
  (114 shorter events, 126.0 us)
Async XLA Ops:
  0.0 1.6 copy-start.1
  0.0 7.1 %copy-start = (f32[32,2048]{1,0:T(8,128)S(1)}, f32[32,2048]{1,0:T(8,128)}, u32[]{:S(2)}) copy-start(f32[32,2048]{1,0:T(8,128)} %param.43) | copy-start | bytes 786436
  8.6 20.8 %collective-permute-start.18 = (f32[64,2048]{1,0:T(8,128)}, f32[64,2048]{1,0:T(8,128)S(1)}, u32[]{:S(2)}, u32[]{:S(2)}) collective-permute-start(f32[64,2048]{1,0:T(8,128)} %get-tuple-element.351), channel_id=1, source_target_pairs={{0,4},{4,0},{1,5},{5,1},{2,6},{6,2},{3,7},{7,3},{8,12},{12,8},{9,1... | collective-permute-start | bytes 1572872 | tf_op jit(solution)/shard_map/cond/branch_1_fun/ppermute | solution.py:19
  12.2 16.5 %collective-permute-start.19 = (f32[32,2048]{1,0:T(8,128)}, f32[32,2048]{1,0:T(8,128)S(1)}, u32[]{:S(2)}, u32[]{:S(2)}) collective-permute-start(f32[32,2048]{1,0:T(8,128)} %get-tuple-element.352), channel_id=1, source_target_pairs={{0,4},{4,0},{1,5},{5,1},{2,6},{6,2},{3,7},{7,3},{8,12},{12,8},{9,1... | collective-permute-start | bytes 786440 | tf_op jit(solution)/shard_map/cond/branch_1_fun/ppermute | solution.py:19
  30.2 20.9 %collective-permute-start.22 = (f32[64,2048]{1,0:T(8,128)}, f32[64,2048]{1,0:T(8,128)S(1)}, u32[]{:S(2)}, u32[]{:S(2)}) collective-permute-start(f32[64,2048]{1,0:T(8,128)} %get-tuple-element.355), channel_id=1, source_target_pairs={{0,16},{16,0},{1,17},{17,1},{2,18},{18,2},{3,19},{19,3},{4,20},{20... | collective-permute-start | bytes 1572872 | tf_op jit(solution)/shard_map/cond/branch_1_fun/ppermute | solution.py:19
  34.0 16.4 %collective-permute-start.23 = (f32[32,2048]{1,0:T(8,128)}, f32[32,2048]{1,0:T(8,128)S(1)}, u32[]{:S(2)}, u32[]{:S(2)}) collective-permute-start(f32[32,2048]{1,0:T(8,128)} %get-tuple-element.356), channel_id=1, source_target_pairs={{0,16},{16,0},{1,17},{17,1},{2,18},{18,2},{3,19},{19,3},{4,20},{20... | collective-permute-start | bytes 786440 | tf_op jit(solution)/shard_map/cond/branch_1_fun/ppermute | solution.py:19
  153.7 19.2 %collective-permute-start.4 = (f32[64,2048]{1,0:T(8,128)}, f32[64,2048]{1,0:T(8,128)S(1)}, u32[]{:S(2)}, u32[]{:S(2)}) collective-permute-start(f32[64,2048]{1,0:T(8,128)} %get-tuple-element.326), channel_id=1, source_target_pairs={{0,4},{4,0},{1,5},{5,1},{2,6},{6,2},{3,7},{7,3},{8,12},{12,8},{9,1... | collective-permute-start | bytes 1572872 | tf_op jit(solution)/shard_map/cond/branch_1_fun/ppermute | solution.py:19
  156.4 15.8 %collective-permute-start.5 = (f32[32,2048]{1,0:T(8,128)}, f32[32,2048]{1,0:T(8,128)S(1)}, u32[]{:S(2)}, u32[]{:S(2)}) collective-permute-start(f32[32,2048]{1,0:T(8,128)} %get-tuple-element.327), channel_id=1, source_target_pairs={{0,4},{4,0},{1,5},{5,1},{2,6},{6,2},{3,7},{7,3},{8,12},{12,8},{9,1... | collective-permute-start | bytes 786440 | tf_op jit(solution)/shard_map/cond/branch_1_fun/ppermute | solution.py:19
  173.7 18.2 %collective-permute-start.8 = (f32[64,2048]{1,0:T(8,128)}, f32[64,2048]{1,0:T(8,128)S(1)}, u32[]{:S(2)}, u32[]{:S(2)}) collective-permute-start(f32[64,2048]{1,0:T(8,128)} %get-tuple-element.330), channel_id=1, source_target_pairs={{0,16},{16,0},{1,17},{17,1},{2,18},{18,2},{3,19},{19,3},{4,20},{20... | collective-permute-start | bytes 1572872 | tf_op jit(solution)/shard_map/cond/branch_1_fun/ppermute | solution.py:19
  176.3 14.9 %collective-permute-start.9 = (f32[32,2048]{1,0:T(8,128)}, f32[32,2048]{1,0:T(8,128)S(1)}, u32[]{:S(2)}, u32[]{:S(2)}) collective-permute-start(f32[32,2048]{1,0:T(8,128)} %get-tuple-element.331), channel_id=1, source_target_pairs={{0,16},{16,0},{1,17},{17,1},{2,18},{18,2},{3,19},{19,3},{4,20},{20... | collective-permute-start | bytes 786440 | tf_op jit(solution)/shard_map/cond/branch_1_fun/ppermute | solution.py:19
  192.7 36.9 %collective-permute-start.12 = (f32[64,2048]{1,0:T(8,128)}, f32[64,2048]{1,0:T(8,128)S(1)}, u32[]{:S(2)}, u32[]{:S(2)}) collective-permute-start(f32[64,2048]{1,0:T(8,128)} %get-tuple-element.334), channel_id=1, source_target_pairs={{0,64},{64,0},{1,65},{65,1},{2,66},{66,2},{3,67},{67,3},{4,68},{68... | collective-permute-start | bytes 1572872 | tf_op jit(solution)/shard_map/cond/branch_1_fun/ppermute | solution.py:19
  195.2 33.6 %collective-permute-start.13 = (f32[32,2048]{1,0:T(8,128)}, f32[32,2048]{1,0:T(8,128)S(1)}, u32[]{:S(2)}, u32[]{:S(2)}) collective-permute-start(f32[32,2048]{1,0:T(8,128)} %get-tuple-element.335), channel_id=1, source_target_pairs={{0,64},{64,0},{1,65},{65,1},{2,66},{66,2},{3,67},{67,3},{4,68},{68... | collective-permute-start | bytes 786440 | tf_op jit(solution)/shard_map/cond/branch_1_fun/ppermute | solution.py:19
  230.4 42.1 %collective-permute-start.28 = (f32[64,2048]{1,0:T(8,128)}, f32[64,2048]{1,0:T(8,128)S(1)}, u32[]{:S(2)}, u32[]{:S(2)}) collective-permute-start(f32[64,2048]{1,0:T(8,128)} %get-tuple-element.338), channel_id=1, source_target_pairs={{0,128},{128,0},{1,129},{129,1},{2,130},{130,2},{3,131},{131,3},{4... | collective-permute-start | bytes 1572872 | tf_op jit(solution)/shard_map/cond/branch_1_fun/ppermute | solution.py:19
  237.6 34.2 %collective-permute-start.29 = (f32[32,2048]{1,0:T(8,128)}, f32[32,2048]{1,0:T(8,128)S(1)}, u32[]{:S(2)}, u32[]{:S(2)}) collective-permute-start(f32[32,2048]{1,0:T(8,128)} %get-tuple-element.339), channel_id=1, source_target_pairs={{0,128},{128,0},{1,129},{129,1},{2,130},{130,2},{3,131},{131,3},{4... | collective-permute-start | bytes 786440 | tf_op jit(solution)/shard_map/cond/branch_1_fun/ppermute | solution.py:19
where the time goes:
time: 331 us; the launch traced here: 329 us
  matrix products  147 us (44%)
  waiting for transfers between devices  131 us (40%)
  starting transfers between devices  23.1 us (7%)
  local copies, waits for them, and re-layouts  13.6 us (4%)
  between operations  10.2 us (3%)
    ppermute x12, waiting for transfers between devices, partner(): return lax.ppermute(block, axis, route)  131 us
    dot_general x24, matrix products, matern(): lax.dot_general(left, right, (((0,), (0,)), ((), ())), precision=lax.Prec...  78.9 us
    dot_general x24, matrix products, one_piece(): lax.dot_general(weights, kernel, (((1,), (1,)), ((), ())), precision=lax....  68.3 us
    ppermute x12, starting transfers between devices, partner(): return lax.ppermute(block, axis, route)  23.1 us
    cond x16, local copies, waits for them, and re-layouts  11.9 us
  transfers between devices with their start and end apart: 12, of which 6 were waited for; matrix products, arithmetic and copies ran while one was open for 1% of the time, Pallas kernels for 0%

commit v1 on v0

v1 whole, which is shorter than its diff:
```python
import math

import jax
import jax.experimental.pallas as pl
import jax.experimental.pallas.tpu as pltpu
import jax.numpy as jnp
from jax import lax
from jax.sharding import PartitionSpec as P

N = 256
FEAT = 64
PROBES = 32
BLK = 2048
ROUNDS = 2
ROWS = 6
GROUPS = (FEAT + PROBES) // ROWS
MESH = pl.DeviceIdType.MESH

LN2 = math.log(2.0)
COORD = math.sqrt(5.0) / LN2
ALPHA = 3.0 / LN2
BETA = 3.0 / LN2**2
GAMMA = LN2**2 / 3.0

TP = 2048
TQ = 256
f32 = jnp.float32
bf16 = jnp.bfloat16


def split(x):
    high = x.astype(bf16)
    return high, (x - high.astype(f32)).astype(bf16)


def set_right(cat, right, right_sq, weights):
    high, low = split(cat[:FEAT, :])
    rounded = high.astype(f32) + low.astype(f32)
    right[...] = jnp.concatenate([high, low, high, low], 0)
    right_sq[...] = jnp.sum(rounded * rounded, axis=0, keepdims=True)
    high, low = split(cat[FEAT:, :])
    weights[...] = jnp.concatenate([high, low], 0)


def set_left(cat, left, left_sq):
    high, low = split(cat[:FEAT, :].T)
    rounded = high.astype(f32) + low.astype(f32)
    left_sq[...] = jnp.sum(rounded * rounded, axis=1, keepdims=True)
    high, low = high * bf16(-2), low * bf16(-2)
    left[...] = jnp.concatenate([high, high, low, low], 1)


def add_block(left, left_sq, right, right_sq, weights, total):
    n_p = BLK // TP

    def step(i, carry):
        ps = pl.ds(pl.multiple_of(lax.rem(i, n_p) * TP, TP), TP)
        qs = pl.ds(pl.multiple_of((i // n_p) * TQ, TQ), TQ)
        inner = jnp.dot(left[ps, :], right[:, qs], preferred_element_type=f32)
        d = jnp.maximum((inner + left_sq[ps, :]) + right_sq[:, qs], 1e-30)
        t = d * lax.rsqrt(d)
        k = ((d + BETA) + ALPHA * t) * jnp.exp2(-t)
        high, low = split(k)
        w = weights[:, qs]
        dims = (((1,), (1,)), ((), ()))
        total[ps, :] += lax.dot_general(high, w, dims, preferred_element_type=f32) + lax.dot_general(
            low, w, dims, preferred_element_type=f32
        )
        return carry

    lax.fori_loop(0, n_p * (BLK // TQ), step, 0)


def kernel(
    partners, points, probes, inv_length, out,
    cat, stage, mid, send, recv, left, left_sq, right, right_sq, weights, total,
    spread_send, spread_recv, deliver_send, deliver_recv,
):
    me = lax.axis_index("pts")

    def target(d):
        return lax.rem(me + lax.rem(d, 8) * 32 + d // 8, N)

    barrier = pltpu.get_barrier_semaphore()

    @pl.loop(1, N)
    def _(d):
        pl.semaphore_signal(barrier, inc=1, device_id=(target(d),), device_id_type=MESH)

    cat[:FEAT, :] = points[...] * (inv_length[...] * COORD)
    cat[FEAT:, :] = probes[...]

    @pl.loop(0, BLK // 128)
    def _(c):
        columns = pl.ds(pl.multiple_of(c * 128, 128), 128)
        for g in range(GROUPS):
            stage[c * GROUPS + g] = cat[g * ROWS : (g + 1) * ROWS, columns]

    pl.semaphore_wait(barrier, N - 1)

    @pl.loop(1, N)
    def _(d):
        t = target(d)
        pltpu.make_async_remote_copy(
            src_ref=stage.at[t], dst_ref=mid.at[me], send_sem=spread_send, recv_sem=spread_recv,
            device_id=(t,), device_id_type=MESH,
        ).start()

    mid[me] = stage[me]

    total[...] = jnp.zeros_like(total)
    set_right(cat, right, right_sq, weights)
    set_left(cat, left, left_sq)
    add_block(left, left_sq, right, right_sq, weights, total)

    most = pl.ds(0, N - 1)
    pltpu.make_async_copy(mid.at[most], mid.at[most], spread_recv).wait()

    for r in range(ROUNDS):

        @pl.loop(1, N)
        def _(d):
            t = target(d)
            send[r, t] = mid[partners[r, t]]
            pltpu.make_async_remote_copy(
                src_ref=send.at[r, t], dst_ref=recv.at[r, me], send_sem=deliver_send.at[r],
                recv_sem=deliver_recv.at[r], device_id=(t,), device_id_type=MESH,
            ).start()

        recv[r, me] = mid[partners[r, me]]

    for r in range(ROUNDS):
        pltpu.make_async_copy(recv.at[r, most], recv.at[r, most], deliver_recv.at[r]).wait()

        @pl.loop(0, BLK // 128)
        def _(c):
            columns = pl.ds(pl.multiple_of(c * 128, 128), 128)
            for g in range(GROUPS):
                cat[g * ROWS : (g + 1) * ROWS, columns] = recv[r, c * GROUPS + g]

        set_right(cat, right, right_sq, weights)
        add_block(left, left_sq, right, right_sq, weights, total)

    pltpu.make_async_copy(stage.at[most], stage.at[most], spread_send).wait()
    for r in range(ROUNDS):
        pltpu.make_async_copy(send.at[r, most], send.at[r, most], deliver_send.at[r]).wait()
    sums = total[...]
    out[...] = ((sums[:, :PROBES] + sums[:, PROBES:]) * GAMMA).T


def body(points, probes, inv_length, partners):
    vmem = pl.BlockSpec(memory_space=pltpu.VMEM)
    return pl.pallas_call(
        kernel,
        out_shape=jax.ShapeDtypeStruct((PROBES, BLK), f32),
        in_specs=[pl.BlockSpec(memory_space=pltpu.SMEM), vmem, vmem, vmem],
        out_specs=vmem,
        scratch_shapes=[
            pltpu.VMEM((FEAT + PROBES, BLK), f32),
            pltpu.VMEM((N, ROWS, 128), f32),
            pltpu.VMEM((N, ROWS, 128), f32),
            pltpu.VMEM((ROUNDS, N, ROWS, 128), f32),
            pltpu.VMEM((ROUNDS, N, ROWS, 128), f32),
            pltpu.VMEM((BLK, 4 * FEAT), bf16),
            pltpu.VMEM((BLK, 1), f32),
            pltpu.VMEM((4 * FEAT, BLK), bf16),
            pltpu.VMEM((1, BLK), f32),
            pltpu.VMEM((2 * PROBES, BLK), bf16),
            pltpu.VMEM((BLK, 2 * PROBES), f32),
            pltpu.SemaphoreType.DMA,
            pltpu.SemaphoreType.DMA,
            pltpu.SemaphoreType.DMA((ROUNDS,)),
            pltpu.SemaphoreType.DMA((ROUNDS,)),
        ],
        compiler_params=pltpu.CompilerParams(collective_id=0, has_side_effects=True, vmem_limit_bytes=48 << 20),
    )(partners, points, probes, inv_length[:, None])


def solution(mesh):
    in_specs = (P(None, "pts"), P(None, "pts"), P(), P())
    return jax.shard_map(body, mesh=mesh, in_specs=in_specs, out_specs=P(None, "pts"), check_vma=False)
```

time: 331 us -> 95.4 us (0.29)
  matrix products: 147 us -> 0 us
  waiting for transfers between devices: 131 us -> 0 us
  Pallas kernels: 0 us -> 91.1 us
  starting transfers between devices: 23.1 us -> 0 us
  between operations: 10.2 us -> 0.01 us
  local copies, waits for them, and re-layouts: 13.6 us -> 4.03 us
    dot_general x48 -> x0, matrix products: 147 us -> none  [the longest x24 78.9 us: matern(): lax.dot_general(left, right, (((0,), (0,)), ((), ())), precision=lax.Prec...]
    ppermute x12 -> x0, waiting for transfers between devices: 131 us -> none  [partner(): return lax.ppermute(block, axis, route)]
    pallas_call x0 -> x1, Pallas kernels: none -> 91.1 us  [body(): pl.pallas_call(kernel, out_shape=jax.ShapeDtypeStruct((PROBES, BLK), f32)...]
    ppermute x12 -> x0, starting transfers between devices: 23.1 us -> none  [partner(): return lax.ppermute(block, axis, route)]
    cond x16 -> x0, local copies, waits for them, and re-layouts: 11.9 us -> none
    unnamed x5 -> x9, local copies, waits for them, and re-layouts: 0.17 us -> 3.94 us
  transfers between devices with their start and end apart: 12 -> 0, of which waited for: 6 -> 0; matrix products, arithmetic and copies ran while one was open for 1% -> 0% of each run, Pallas kernels for 0% -> 0%
where the time goes in v1:
time: 95.4 us; the launch traced here: 95.2 us
  Pallas kernels  91.1 us (95%)
  local copies, waits for them, and re-layouts  4.03 us (4%)
    pallas_call x1, Pallas kernels, body(): pl.pallas_call(kernel, out_shape=jax.ShapeDtypeStruct((PROBES, BLK), f32)...  91.1 us
    unnamed x9, local copies, waits for them, and re-layouts  3.94 us

profile of v1, /device:TPU:1, one launch (start us, length us, event | category | flops | bytes accessed | tf_op | source)
XLA Modules:
  0.0 95.2 jit_solution(8839900157803311049)
XLA Ops:
  0.0 0.0 copy-start.3
  0.0 0.7 copy-done.3
  0.7 0.0 copy-start.2
  0.7 0.1 copy.5.inv_length
  0.8 0.6 copy-done.2
  1.3 0.0 copy-start
  1.3 1.0 %copy-done = f32[64,2048]{1,0:T(8,128)S(1)} copy-done((f32[64,2048]{1,0:T(8,128)S(1)}, f32[64,2048]{1,0:T(8,128)}, u32[]{:S(2)}) %copy-start) | copy-done | bytes 524312
  2.4 0.0 copy-start.1
  2.4 0.9 copy-done.1
  3.3 91.1 %shard_map.46 = f32[32,2048]{1,0:T(8,128)S(1)} custom-call(s32[2,256]{1,0:T(2,128)S(1)} %copy-done.2, f32[64,2048]{1,0:T(8,128)S(1)} %copy-done, f32[32,2048]{1,0:T(8,128)S(1)} %copy-done.1, f32[64,1]{1,0:T(8,128)S(1)} %copy.5.inv_length), custom_call_target="tpu_custom_call" | custom-call | tf_op jit(solution)/shard_map/pallas_call | solution.py:153
  94.5 0.7 copy.7
Async XLA Ops:
  0.0 0.7 copy-start.3
  0.7 0.7 copy-start.2
  1.3 1.0 %copy-start = (f32[64,2048]{1,0:T(8,128)S(1)}, f32[64,2048]{1,0:T(8,128)}, u32[]{:S(2)}) copy-start(f32[64,2048]{1,0:T(8,128)} %points.1) | copy-start | bytes 1572868
  2.4 0.9 copy-start.1

commit v2 on v1

--- a/solution.py
+++ b/solution.py
@@ -22,7 +22,7 @@
 BETA = 3.0 / LN2**2
 GAMMA = LN2**2 / 3.0
 
-TP = 2048
+PARTS = 2
 TQ = 256
 f32 = jnp.float32
 bf16 = jnp.bfloat16
@@ -51,24 +51,26 @@
 
 
 def add_block(left, left_sq, right, right_sq, weights, total):
-    n_p = BLK // TP
+    dims = (((1,), (1,)), ((), ()))
 
     def step(i, carry):
-        ps = pl.ds(pl.multiple_of(lax.rem(i, n_p) * TP, TP), TP)
-        qs = pl.ds(pl.multiple_of((i // n_p) * TQ, TQ), TQ)
-        inner = jnp.dot(left[ps, :], right[:, qs], preferred_element_type=f32)
-        d = jnp.maximum((inner + left_sq[ps, :]) + right_sq[:, qs], 1e-30)
-        t = d * lax.rsqrt(d)
-        k = ((d + BETA) + ALPHA * t) * jnp.exp2(-t)
-        high, low = split(k)
-        w = weights[:, qs]
-        dims = (((1,), (1,)), ((), ()))
-        total[ps, :] += lax.dot_general(high, w, dims, preferred_element_type=f32) + lax.dot_general(
-            low, w, dims, preferred_element_type=f32
-        )
+        sums = None
+        for part in range(PARTS):
+            qs = pl.ds(pl.multiple_of((i * PARTS + part) * TQ, TQ), TQ)
+            inner = jnp.dot(left[...], right[:, qs], preferred_element_type=f32)
+            d = jnp.maximum((inner + left_sq[...]) + right_sq[:, qs], 1e-30)
+            t = d * lax.rsqrt(d)
+            k = ((d + BETA) + ALPHA * t) * jnp.exp2(-t)
+            high, low = split(k)
+            w = weights[:, qs]
+            term = lax.dot_general(high, w, dims, preferred_element_type=f32) + lax.dot_general(
+                low, w, dims, preferred_element_type=f32
+            )
+            sums = term if sums is None else sums + term
+        total[...] += sums
         return carry
 
-    lax.fori_loop(0, n_p * (BLK // TQ), step, 0)
+    lax.fori_loop(0, BLK // (PARTS * TQ), step, 0)
 
 
 def kernel(
@@ -87,7 +89,8 @@
     def _(d):
         pl.semaphore_signal(barrier, inc=1, device_id=(target(d),), device_id_type=MESH)
 
-    cat[:FEAT, :] = points[...] * (inv_length[...] * COORD)
+    scale = jnp.broadcast_to(inv_length[...] * COORD, (8, FEAT)).T[:, :1]
+    cat[:FEAT, :] = points[...] * scale
     cat[FEAT:, :] = probes[...]
 
     @pl.loop(0, BLK // 128)
@@ -172,8 +175,8 @@
             pltpu.SemaphoreType.DMA((ROUNDS,)),
             pltpu.SemaphoreType.DMA((ROUNDS,)),
         ],
-        compiler_params=pltpu.CompilerParams(collective_id=0, has_side_effects=True, vmem_limit_bytes=48 << 20),
-    )(partners, points, probes, inv_length[:, None])
+        compiler_params=pltpu.CompilerParams(collective_id=0, has_side_effects=True, vmem_limit_bytes=62 << 20),
+    )(partners, points, probes, inv_length[None, :])
 
 
 def solution(mesh):

time: 95.4 us -> 90.2 us (0.945)
  Pallas kernels: 91.1 us -> 88.4 us
  local copies, waits for them, and re-layouts: 4.03 us -> 1.67 us
    pallas_call x1, Pallas kernels: 91.1 us -> 88.4 us  [body(): pl.pallas_call(kernel, out_shape=jax.ShapeDtypeStruct((PROBES, BLK), f32)...]
    unnamed x9 -> x1, local copies, waits for them, and re-layouts: 3.94 us -> 1.67 us
where the time goes in v2:
time: 90.2 us; the launch traced here: 90.1 us
  Pallas kernels  88.4 us (98%)
  local copies, waits for them, and re-layouts  1.67 us (2%)
    pallas_call x1, Pallas kernels, body(): pl.pallas_call(kernel, out_shape=jax.ShapeDtypeStruct((PROBES, BLK), f32)...  88.4 us

profile of v2, /device:TPU:1, one launch (start us, length us, event | category | flops | bytes accessed | tf_op | source)
XLA Modules:
  0.0 90.1 jit_solution(8749979077043440000)
XLA Ops:
  0.0 88.4 %shard_map.46 = f32[32,2048]{1,0:T(8,128)} custom-call(s32[2,256]{1,0:T(2,128)} %partners.1, f32[64,2048]{1,0:T(8,128)} %points.1, f32[32,2048]{1,0:T(8,128)} %probes.1, f32[1,64]{1,0:T(1,128)} %bitcast.1), custom_call_target="tpu_custom_call" | custom-call | tf_op jit(solution)/shard_map/pallas_call | solution.py:156
  88.4 1.7 %copy.6 = f32[32,2048]{1,0:T(8,128)} copy(f32[32,2048]{1,0:T(8,128)} %shard_map.46) | data formatting | bytes 524288

commit v3 on v2

--- a/solution.py
+++ b/solution.py
@@ -22,7 +22,7 @@
 BETA = 3.0 / LN2**2
 GAMMA = LN2**2 / 3.0
 
-PARTS = 2
+PARTS = 4
 TQ = 256
 f32 = jnp.float32
 bf16 = jnp.bfloat16
@@ -84,20 +84,23 @@
         return lax.rem(me + lax.rem(d, 8) * 32 + d // 8, N)
 
     barrier = pltpu.get_barrier_semaphore()
-
-    @pl.loop(1, N)
-    def _(d):
-        pl.semaphore_signal(barrier, inc=1, device_id=(target(d),), device_id_type=MESH)
-
     scale = jnp.broadcast_to(inv_length[...] * COORD, (8, FEAT)).T[:, :1]
     cat[:FEAT, :] = points[...] * scale
     cat[FEAT:, :] = probes[...]
 
-    @pl.loop(0, BLK // 128)
-    def _(c):
+    def put(c):
         columns = pl.ds(pl.multiple_of(c * 128, 128), 128)
         for g in range(GROUPS):
             stage[c * GROUPS + g] = cat[g * ROWS : (g + 1) * ROWS, columns]
+
+    @pl.loop(0, 15)
+    def _(c):
+        for g in range(17):
+            t = lax.rem(me + (c * 17 + g + 1), N)
+            pl.semaphore_signal(barrier, inc=1, device_id=(t,), device_id_type=MESH)
+        put(c)
+
+    put(15)
 
     pl.semaphore_wait(barrier, N - 1)
 
@@ -175,7 +178,7 @@
             pltpu.SemaphoreType.DMA((ROUNDS,)),
             pltpu.SemaphoreType.DMA((ROUNDS,)),
         ],
-        compiler_params=pltpu.CompilerParams(collective_id=0, has_side_effects=True, vmem_limit_bytes=62 << 20),
+        compiler_params=pltpu.CompilerParams(collective_id=0, has_side_effects=True, vmem_limit_bytes=60 << 20),
     )(partners, points, probes, inv_length[None, :])
 
 

time: 90.2 us -> 88.1 us (0.977)
  Pallas kernels: 88.4 us -> 86.3 us
    pallas_call x1, Pallas kernels: 88.4 us -> 86.3 us  [body(): pl.pallas_call(kernel, out_shape=jax.ShapeDtypeStruct((PROBES, BLK), f32)...]
where the time goes in v3:
time: 88.1 us; the launch traced here: 88 us
  Pallas kernels  86.3 us (98%)
  local copies, waits for them, and re-layouts  1.67 us (2%)
    pallas_call x1, Pallas kernels, body(): pl.pallas_call(kernel, out_shape=jax.ShapeDtypeStruct((PROBES, BLK), f32)...  86.3 us

profile of v3, /device:TPU:1, one launch (start us, length us, event | category | flops | bytes accessed | tf_op | source)
XLA Modules:
  0.0 88.0 jit_solution(8189541307237688368)
XLA Ops:
  0.0 86.3 %shard_map.46 = f32[32,2048]{1,0:T(8,128)} custom-call(s32[2,256]{1,0:T(2,128)} %partners.1, f32[64,2048]{1,0:T(8,128)} %points.1, f32[32,2048]{1,0:T(8,128)} %probes.1, f32[1,64]{1,0:T(1,128)} %bitcast.1), custom_call_target="tpu_custom_call" | custom-call | tf_op jit(solution)/shard_map/pallas_call | solution.py:159
  86.3 1.7 %copy.6 = f32[32,2048]{1,0:T(8,128)} copy(f32[32,2048]{1,0:T(8,128)} %shard_map.46) | data formatting | bytes 524288

commit v4 on v1

v4 whole, which is shorter than its diff:
```python
import math

import jax
import jax.experimental.pallas as pl
import jax.experimental.pallas.tpu as pltpu
import jax.numpy as jnp
from jax import lax
from jax.sharding import PartitionSpec as P

N = 256
FEAT = 64
PROBES = 32
BLK = 2048
HALVES = 2
HALF = BLK // HALVES
ROWS = 3
GROUPS = (FEAT + PROBES) // ROWS
MESH = pl.DeviceIdType.MESH

LN2 = math.log(2.0)
COORD = math.sqrt(5.0) / LN2
ALPHA = 3.0 / LN2
BETA = 3.0 / LN2**2
GAMMA = LN2**2 / 3.0

TQ = 256
f32 = jnp.float32
bf16 = jnp.bfloat16


def split(x):
    high = x.astype(bf16)
    return high, (x - high.astype(f32)).astype(bf16)


def set_left(block, left, left_sq):
    high, low = split(block[:FEAT, :].T)
    rounded = high.astype(f32) + low.astype(f32)
    left_sq[...] = jnp.sum(rounded * rounded, axis=1, keepdims=True)
    high, low = high * bf16(-2), low * bf16(-2)
    left[...] = jnp.concatenate([high, high, low, low], 1)


def add_half(block, left, left_sq, right, right_sq, weights, total):
    high, low = split(block[:FEAT, :])
    rounded = high.astype(f32) + low.astype(f32)
    right[...] = jnp.concatenate([high, low, high, low], 0)
    right_sq[...] = jnp.sum(rounded * rounded, axis=0, keepdims=True)
    high, low = split(block[FEAT:, :])
    weights[...] = jnp.concatenate([high, low], 0)

    dims = (((1,), (1,)), ((), ()))
    sums = None
    for part in range(HALF // TQ):
        qs = pl.ds(part * TQ, TQ)
        inner = jnp.dot(left[...], right[:, qs], preferred_element_type=f32)
        d = jnp.maximum((inner + left_sq[...]) + right_sq[:, qs], 1e-30)
        t = d * lax.rsqrt(d)
        k = ((d + BETA) + ALPHA * t) * jnp.exp2(-t)
        high, low = split(k)
        w = weights[:, qs]
        term = lax.dot_general(high, w, dims, preferred_element_type=f32) + lax.dot_general(
            low, w, dims, preferred_element_type=f32
        )
        sums = term if sums is None else sums + term
    total[...] += sums


def kernel(
    partners, points, probes, inv_length, out,
    own, far, stage, mid, send0, recv0, send1, recv1, left, left_sq, right, right_sq, weights, total,
    spread_send, spread_recv, send0_sem, recv0_sem, send1_sem, recv1_sem,
):
    me = lax.axis_index("pts")
    operands = (left, left_sq, right, right_sq, weights, total)

    def target(d):
        return lax.rem(me + lax.rem(d, 8) * 32 + d // 8, N)

    barrier = pltpu.get_barrier_semaphore()
    scale = jnp.broadcast_to(inv_length[...] * COORD, (8, FEAT)).T[:, :1]
    for h in range(HALVES):
        own[h, :FEAT] = points[:, h * HALF : (h + 1) * HALF] * scale
        own[h, FEAT:] = probes[:, h * HALF : (h + 1) * HALF]

    def put(c, h):
        columns = pl.ds(pl.multiple_of(c * 128, 128), 128)
        for g in range(GROUPS):
            stage[c * GROUPS + g, h] = own[h, g * ROWS : (g + 1) * ROWS, columns]

    @pl.loop(0, 15)
    def _(i):
        for g in range(17):
            t = lax.rem(me + (i * 17 + g + 1), N)
            pl.semaphore_signal(barrier, inc=1, device_id=(t,), device_id_type=MESH)
        put(i // 2, lax.rem(i, 2))

    put(7, 1)

    pl.semaphore_wait(barrier, N - 1)

    @pl.loop(1, N)
    def _(d):
        t = target(d)
        pltpu.make_async_remote_copy(
            src_ref=stage.at[t], dst_ref=mid.at[me], send_sem=spread_send, recv_sem=spread_recv,
            device_id=(t,), device_id_type=MESH,
        ).start()

    mid[me] = stage[me]

    total[...] = jnp.zeros_like(total)
    for h in range(HALVES):
        rows = pl.ds(h * HALF, HALF)
        set_left(own.at[h], left.at[rows], left_sq.at[rows])

    @pl.loop(0, HALVES)
    def _(h):
        add_half(own.at[h], *operands)

    most = pl.ds(0, N - 1)
    pltpu.make_async_copy(mid.at[most], mid.at[most], spread_recv).wait()

    @pl.loop(1, N)
    def _(d):
        t = target(d)
        send0[t] = mid[partners[0, t]]
        pltpu.make_async_remote_copy(
            src_ref=send0.at[t], dst_ref=recv0.at[me], send_sem=send0_sem, recv_sem=recv0_sem,
            device_id=(t,), device_id_type=MESH,
        ).start()

    recv0[me] = mid[partners[0, me]]

    @pl.loop(0, HALVES)
    def _(h):
        @pl.loop(1, N)
        def _(d):
            t = target(d)
            send1[h, t] = mid[partners[1, t], h]
            pltpu.make_async_remote_copy(
                src_ref=send1.at[h, t], dst_ref=recv1.at[h, me], send_sem=send1_sem.at[h], recv_sem=recv1_sem.at[h],
                device_id=(t,), device_id_type=MESH,
            ).start()

        recv1[h, me] = mid[partners[1, me], h]

    pltpu.make_async_copy(recv0.at[most], recv0.at[most], recv0_sem).wait()

    @pl.loop(0, HALVES)
    def _(h):
        @pl.loop(0, HALF // 128)
        def _(c):
            columns = pl.ds(pl.multiple_of(c * 128, 128), 128)
            for g in range(GROUPS):
                far[g * ROWS : (g + 1) * ROWS, columns] = recv0[c * GROUPS + g, h]

        add_half(far, *operands)

    @pl.loop(0, HALVES)
    def _(h):
        pltpu.make_async_copy(recv1.at[h, most], recv1.at[h, most], recv1_sem.at[h]).wait()

        @pl.loop(0, HALF // 128)
        def _(c):
            columns = pl.ds(pl.multiple_of(c * 128, 128), 128)
            for g in range(GROUPS):
                far[g * ROWS : (g + 1) * ROWS, columns] = recv1[h, c * GROUPS + g]

        add_half(far, *operands)

    pltpu.make_async_copy(stage.at[most], stage.at[most], spread_send).wait()
    pltpu.make_async_copy(send0.at[most], send0.at[most], send0_sem).wait()
    for h in range(HALVES):
        pltpu.make_async_copy(send1.at[h, most], send1.at[h, most], send1_sem.at[h]).wait()
    sums = total[...]
    out[...] = ((sums[:, :PROBES] + sums[:, PROBES:]) * GAMMA).T


def body(points, probes, inv_length, partners):
    vmem = pl.BlockSpec(memory_space=pltpu.VMEM)
    return pl.pallas_call(
        kernel,
        out_shape=jax.ShapeDtypeStruct((PROBES, BLK), f32),
        in_specs=[pl.BlockSpec(memory_space=pltpu.SMEM), vmem, vmem, vmem],
        out_specs=vmem,
        scratch_shapes=[
            pltpu.VMEM((HALVES, FEAT + PROBES, HALF), f32),
            pltpu.VMEM((FEAT + PROBES, HALF), f32),
            pltpu.VMEM((N, HALVES, ROWS, 128), f32),
            pltpu.VMEM((N, HALVES, ROWS, 128), f32),
            pltpu.VMEM((N, HALVES, ROWS, 128), f32),
            pltpu.VMEM((N, HALVES, ROWS, 128), f32),
            pltpu.VMEM((HALVES, N, ROWS, 128), f32),
            pltpu.VMEM((HALVES, N, ROWS, 128), f32),
            pltpu.VMEM((BLK, 4 * FEAT), bf16),
            pltpu.VMEM((BLK, 1), f32),
            pltpu.VMEM((4 * FEAT, HALF), bf16),
            pltpu.VMEM((1, HALF), f32),
            pltpu.VMEM((2 * PROBES, HALF), bf16),
            pltpu.VMEM((BLK, 2 * PROBES), f32),
            pltpu.SemaphoreType.DMA,
            pltpu.SemaphoreType.DMA,
            pltpu.SemaphoreType.DMA,
            pltpu.SemaphoreType.DMA,
            pltpu.SemaphoreType.DMA((HALVES,)),
            pltpu.SemaphoreType.DMA((HALVES,)),
        ],
        compiler_params=pltpu.CompilerParams(collective_id=0, has_side_effects=True, vmem_limit_bytes=60 << 20),
    )(partners, points, probes, inv_length[None, :])


def solution(mesh):
    in_specs = (P(None, "pts"), P(None, "pts"), P(), P())
    return jax.shard_map(body, mesh=mesh, in_specs=in_specs, out_specs=P(None, "pts"), check_vma=False)
```

time: 95.4 us -> 83.3 us (0.87)
  Pallas kernels: 91.1 us -> 81.5 us
  local copies, waits for them, and re-layouts: 4.03 us -> 1.67 us
    pallas_call x1, Pallas kernels: 91.1 us -> 81.5 us  [body(): pl.pallas_call(kernel, out_shape=jax.ShapeDtypeStruct((PROBES, BLK), f32)...]
    unnamed x9 -> x1, local copies, waits for them, and re-layouts: 3.94 us -> 1.67 us
where the time goes in v4:
time: 83.3 us; the launch traced here: 83.2 us
  Pallas kernels  81.5 us (98%)
  local copies, waits for them, and re-layouts  1.67 us (2%)
    pallas_call x1, Pallas kernels, body(): pl.pallas_call(kernel, out_shape=jax.ShapeDtypeStruct((PROBES, BLK), f32)...  81.5 us
    unnamed x1, local copies, waits for them, and re-layouts  1.67 us

profile of v4, /device:TPU:1, one launch (start us, length us, event | category | flops | bytes accessed | tf_op | source)
XLA Modules:
  0.0 83.2 jit_solution(1604435428282878207)
XLA Ops:
  0.0 81.5 %shard_map.46 = f32[32,2048]{1,0:T(8,128)} custom-call(s32[2,256]{1,0:T(2,128)} %partners.1, f32[64,2048]{1,0:T(8,128)} %points.1, f32[32,2048]{1,0:T(8,128)} %probes.1, f32[1,64]{1,0:T(1,128)} %bitcast.1), custom_call_target="tpu_custom_call" | custom-call | tf_op jit(solution)/shard_map/pallas_call | solution.py:182
  81.5 1.7 %copy.6 = f32[32,2048]{1,0:T(8,128)} copy(f32[32,2048]{1,0:T(8,128)} %shard_map.46) | data formatting | bytes 524288
